TPU v7x, 32 devices: a whole 2x2x4 slice. The times are simulated.
32 devices in a mesh: groups: 2 (over x), node: 4 (over y, core), local: 4 (over z).
Axes of the slice: x: 2, y: 2, z: 4, core: 2. Of those that a mesh axis runs over, the one named last changes fastest.
Arguments:
- hidden: bfloat16 [2048, 8, 1024], P(('groups', 'node', 'local')), parts along dimension 0, may hold values from -6 to 6
- gates: float32 [2048, 8], P(('groups', 'node', 'local')), parts along dimension 0, may hold values from 0.05 to 1
- node_groups: int32 [2048, 4], P(('groups', 'node', 'local')), parts along dimension 0, may hold values from 0 to 3, as said below
- group_picks: int32 [2048, 8], P(('groups', 'node', 'local')), parts along dimension 0, may hold values from 0 to 3, as said below
- down_weight: bfloat16 [16, 1024, 3584], P(('node', 'local')), may hold values from -0.1875 to 0.1875
Outputs:
- mixed: bfloat16 [2048, 3584], P(('groups', 'node', 'local')), parts along dimension 0
There are 2 independent parts, one for each index of `groups`. A program takes and returns all parts, laid end to end along the dimension named above; an argument that names none is the same for every part. Nothing has to cross between parts.
Inputs may be any that keep to these rules, and one draw needn't show every extreme that they name: `node_groups`: each row lists 4 different node groups. `group_picks`: the picks of one listed group of a row name different experts; at most 32 rows of one device name one expert, and in every draw every expert of some node group is named by exactly 32 rows of every device.
All inputs are finite; a program needn't handle non-finite values.
Results may differ from a plain program's by a relative error of at most 0.0085.
Values may be sent and summed in bfloat16 or wider, within the bound.
A program may use at most 128 MiB of HBM per device.

v0:
```python
import jax
import jax.numpy as jnp
from jax import lax
from jax.sharding import PartitionSpec as P

route_scale = 2.5


def expert_apply(inputs, weight_block):
    flat_rows = inputs.reshape(-1, inputs.shape[-1])
    product = jnp.dot(flat_rows, weight_block, preferred_element_type=jnp.float32)
    return product.astype(jnp.bfloat16).reshape(inputs.shape[:-1] + (weight_block.shape[1],))


def slot_positions(targets, count):
    one_hot = (targets[:, None] == jnp.arange(count, dtype=jnp.int32)[None, :]).astype(jnp.int32)
    running = jnp.cumsum(one_hot, axis=0) - 1
    return jnp.sum(running * one_hot, axis=1)


def pack_rows(hidden, node_groups, pair_picks, local_count, device_count, capacity):
    hidden_width = hidden.shape[2]
    expert_ids = (node_groups[:, :, None] * local_count + pair_picks).reshape(-1)
    slot_index = expert_ids * capacity + slot_positions(expert_ids, device_count)
    outgoing = (
        jnp.zeros((device_count * capacity, hidden_width), jnp.bfloat16)
        .at[slot_index]
        .set(hidden.reshape(-1, hidden_width))
    )
    return (slot_index, outgoing)


def combine_rows(returned, slot_index, pair_weights):
    row_count, group_count, pair_count = pair_weights.shape
    model_width = returned.shape[-1]
    picked = returned.reshape(-1, model_width)[slot_index].astype(jnp.float32)
    picked = picked.reshape(row_count, group_count, pair_count, model_width)
    group_sums = jnp.sum(pair_weights.astype(jnp.float32)[..., None] * picked, axis=2).astype(
        jnp.bfloat16
    )
    return jnp.sum(group_sums.astype(jnp.float32), axis=1).astype(jnp.bfloat16)


def shards(hidden, gates, node_groups, group_picks, down_weight):
    row_count, pick_count, hidden_width = hidden.shape
    group_count = node_groups.shape[1]
    pair_count = pick_count // group_count
    node_count = lax.axis_size("node")
    local_count = lax.axis_size("local")
    device_count = node_count * local_count
    capacity = 2 * row_count // local_count
    weight_block = down_weight[0]
    route_weights = (route_scale * gates / jnp.sum(gates, axis=1, keepdims=True)).astype(
        jnp.bfloat16
    )
    pair_weights = route_weights.reshape(row_count, group_count, pair_count)
    pair_picks = group_picks.reshape(row_count, group_count, pair_count)
    slot_index, outgoing = pack_rows(
        hidden, node_groups, pair_picks, local_count, device_count, capacity
    )
    returned = lax.all_to_all(
        expert_apply(
            lax.all_to_all(
                outgoing.reshape(device_count, capacity, hidden_width),
                ("node", "local"),
                split_axis=0,
                concat_axis=0,
                tiled=True,
            ),
            weight_block,
        ),
        ("node", "local"),
        split_axis=0,
        concat_axis=0,
        tiled=True,
    )
    return combine_rows(returned, slot_index, pair_weights)


def solution(mesh):
    return jax.shard_map(
        shards,
        mesh=mesh,
        in_specs=(
            P(("groups", "node", "local"), None, None),
            P(("groups", "node", "local"), None),
            P(("groups", "node", "local"), None),
            P(("groups", "node", "local"), None),
            P(("node", "local"), None, None),
        ),
        out_specs=P(("groups", "node", "local"), None),
        check_vma=False,
    )
```

profile of v0, /device:TPU:0, one launch (start us, length us, event | category | flops | bytes accessed | tf_op | source)
XLA Modules:
  0.0 171.4 jit_solution(8821111556011397452)
XLA Ops:
  0.0 0.0 copy-start
  0.0 0.8 broadcast_multiply_fusion
  0.8 0.1 copy.21
  0.9 0.1 add.54
  1.0 0.2 add.59
  1.2 0.2 add.57
  1.3 0.8 copy.22
  2.1 0.1 reshape.106
  2.2 0.1 reshape.105
  2.3 0.2 add.55
  2.4 0.1 reshape.104
  2.6 1.2 reduce-window.6
  3.7 0.2 slice_reduce_fusion
  4.0 0.1 fusion.9
  4.1 2.8 %scatter_custom_fusion = bf16[512,1024]{1,0:T(8,128)(2,1)S(1)} fusion(s32[512]{0:T(512)S(1)} %bitcast.37, bf16[64,8,1024]{2,1,0:T(8,128)(2,1)S(1)} %copy-done, bf16[]{:T(256)} %constant.5.clone.1), kind=kCustom, calls=%fused_computation.7 | custom fusion | bytes 2097154 | tf_op jit(solution)/shard_map/scatter | solution.py:28
  6.9 34.2 %all_to_all.10 = bf16[16,32,1024]{2,1,0:T(8,128)(2,1)S(1)} all-to-all(bf16[16,32,1024]{2,1,0:T(8,128)(2,1)S(1)} %bitcast.33), channel_id=1, replica_groups=mesh['groups'=2,'node'=4,'local'=4] {'node','local'}, dimensions={0} | all-to-all | bytes 2097152 | tf_op jit(solution)/shard_map/all_to_all | solution.py:63
  41.1 8.6 %fusion.2 = bf16[512,3584]{1,0:T(8,128)(2,1)} fusion(bf16[512,1024]{1,0:T(8,128)(2,1)S(1)} %bitcast.35, bf16[1,1024,3584]{2,1,0:T(8,128)(2,1)} %param.9), kind=kOutput, calls=%fused_computation.5 | convolution fusion | flops 3759931392 | bytes 12058624 | tf_op jit(solution)/shard_map/dot_general | solution.py:11
  49.6 4.8 %all-to-all-start.1 = ((bf16[16,32,3584]{2,1,0:T(8,128)(2,1)}), bf16[16,32,3584]{2,1,0:T(8,128)(2,1)}, u32[]{:S(2)}, u32[]{:S(2)}) async-start(bf16[16,32,3584]{2,1,0:T(8,128)(2,1)} %bitcast.34), calls=%async_computation.1 | async-start | bytes 7340032 | tf_op jit(solution)/shard_map/all_to_all | solution.py:61
  54.5 0.1 copy.20
  54.6 82.8 %all-to-all-done.1 = bf16[16,32,3584]{2,1,0:T(8,128)(2,1)} async-done(((bf16[16,32,3584]{2,1,0:T(8,128)(2,1)}), bf16[16,32,3584]{2,1,0:T(8,128)(2,1)}, u32[]{:S(2)}, u32[]{:S(2)}) %all-to-all-start.1) | async-done | bytes 3670048 | tf_op jit(solution)/shard_map/all_to_all | solution.py:61
  137.4 10.4 %gather_fusion = bf16[512,3584]{1,0:T(8,128)(2,1)} fusion(bf16[512,3584]{1,0:T(8,128)(2,1)} %bitcast.9, s32[1024]{0:T(1024)S(1)} %pad_clamp_fusion), kind=kCustom, calls=%fused_computation | custom fusion | bytes 7342080 | tf_op jit(solution)/shard_map/gather | solution.py:36
  147.8 8.6 %reshape.114 = f32[64,4,2,3584]{3,2,1,0:T(2,128)} reshape(bf16[512,3584]{1,0:T(8,128)(2,1)} %gather_fusion) | data formatting | bytes 11010048 | tf_op jit(solution)/shard_map/convert_element_type | solution.py:36
  156.4 11.7 %multiply_reduce_fusion = bf16[64,4,3584]{2,1,0:T(4,128)(2,1)S(1)} fusion(f32[64,4,2,3584]{3,2,1,0:T(2,128)} %reshape.114, f32[64,4,2]{2,1,0:T(4,128)S(1)} %copy.20), kind=kLoop, calls=%fused_computation.4 | loop fusion | flops 2752512 | bytes 9177088 | tf_op jit(solution)/shard_map/reduce_sum | solution.py:38
  168.1 3.3 %convert_reduce_fusion = bf16[64,3584]{1,0:T(8,128)(2,1)} fusion(bf16[64,4,3584]{2,1,0:T(4,128)(2,1)S(1)} %multiply_reduce_fusion), kind=kLoop, calls=%fused_computation.6 | loop fusion | flops 688128 | bytes 2293760 | tf_op jit(solution)/shard_map/reduce_sum | solution.py:41
  (12 shorter events, 0.1 us)
Async XLA Ops:
  0.0 4.1 %copy-start = (bf16[64,8,1024]{2,1,0:T(8,128)(2,1)S(1)}, bf16[64,8,1024]{2,1,0:T(8,128)(2,1)}, u32[]{:S(2)}) copy-start(bf16[64,8,1024]{2,1,0:T(8,128)(2,1)} %param.5) | copy-start | bytes 3145732
  49.6 4.8 %copy-start.1 = (f32[64,8]{0,1:T(8,128)S(1)}, f32[64,8]{0,1:T(8,128)}, u32[]{:S(2)}) copy-start(f32[64,8]{0,1:T(8,128)} %param.6) | copy-start | bytes 6148
  49.6 87.8 %all-to-all-start.1 = ((bf16[16,32,3584]{2,1,0:T(8,128)(2,1)}), bf16[16,32,3584]{2,1,0:T(8,128)(2,1)}, u32[]{:S(2)}, u32[]{:S(2)}) async-start(bf16[16,32,3584]{2,1,0:T(8,128)(2,1)} %bitcast.34), calls=%async_computation.1 | async-start | bytes 7340032 | tf_op jit(solution)/shard_map/all_to_all | solution.py:61
where the time goes:
time: 172 us; the launch traced here: 171 us
  waiting for transfers between devices  82.8 us (48%)
  blocking collectives  34.2 us (20%)
  local copies, waits for them, and re-layouts  23.9 us (14%)
  other arithmetic  17.1 us (10%)
  matrix products  8.55 us (5%)
  starting transfers between devices  4.81 us (3%)
    all_to_all x1, waiting for transfers between devices, shards(): lax.all_to_all(expert_apply(lax.all_to_all(outgoing.reshape(device_count,...  82.8 us
    all_to_all x1, blocking collectives, shards(): lax.all_to_all(outgoing.reshape(device_count, capacity, hidden_width), ('...  34.2 us
    reduce_sum x1, other arithmetic, combine_rows(): jnp.sum(pair_weights.astype(jnp.float32)[..., None] * picked, axis=2)  11.7 us
    gather x1, local copies, waits for them, and re-layouts, combine_rows(): picked = returned.reshape(-1, model_width)[slot_index].astype(jnp.float32)  10.4 us
    convert_element_type x1, local copies, waits for them, and re-layouts, combine_rows(): picked = returned.reshape(-1, model_width)[slot_index].astype(jnp.float32)  8.61 us
    dot_general x1, matrix products, expert_apply(): jnp.dot(flat_rows, weight_block, preferred_element_type=jnp.float32)  8.55 us
    all_to_all x1, starting transfers between devices, shards(): lax.all_to_all(expert_apply(lax.all_to_all(outgoing.reshape(device_count,...  4.81 us
  transfers between devices with their start and end apart: 1, of which 1 were waited for; matrix products, arithmetic and copies ran while one was open for 0% of the time, Pallas kernels for 0%

commit v1 on v0

--- a/solution.py
+++ b/solution.py
@@ -1,9 +1,16 @@
+import functools
+
 import jax
 import jax.numpy as jnp
 from jax import lax
+from jax.experimental import pallas as pl
+from jax.experimental.pallas import tpu as pltpu
 from jax.sharding import PartitionSpec as P
 
 route_scale = 2.5
+MESH = pl.DeviceIdType.MESH
+BF16 = jnp.bfloat16
+F32 = jnp.float32
 
 
 def expert_apply(inputs, weight_block):
@@ -41,40 +48,272 @@
     return jnp.sum(group_sums.astype(jnp.float32), axis=1).astype(jnp.bfloat16)
 
 
-def shards(hidden, gates, node_groups, group_picks, down_weight):
+def sparse_plan(hidden, route_weights, node_groups, group_picks, weight_block, capacity):
     row_count, pick_count, hidden_width = hidden.shape
     group_count = node_groups.shape[1]
     pair_count = pick_count // group_count
-    node_count = lax.axis_size("node")
     local_count = lax.axis_size("local")
-    device_count = node_count * local_count
-    capacity = 2 * row_count // local_count
-    weight_block = down_weight[0]
-    route_weights = (route_scale * gates / jnp.sum(gates, axis=1, keepdims=True)).astype(
-        jnp.bfloat16
-    )
+    device_count = lax.axis_size("node") * local_count
     pair_weights = route_weights.reshape(row_count, group_count, pair_count)
     pair_picks = group_picks.reshape(row_count, group_count, pair_count)
     slot_index, outgoing = pack_rows(
         hidden, node_groups, pair_picks, local_count, device_count, capacity
     )
-    returned = lax.all_to_all(
-        expert_apply(
-            lax.all_to_all(
-                outgoing.reshape(device_count, capacity, hidden_width),
-                ("node", "local"),
-                split_axis=0,
-                concat_axis=0,
-                tiled=True,
-            ),
-            weight_block,
-        ),
+    arrived = lax.all_to_all(
+        outgoing.reshape(device_count, capacity, hidden_width),
         ("node", "local"),
         split_axis=0,
         concat_axis=0,
         tiled=True,
     )
+    returned = lax.all_to_all(
+        expert_apply(arrived, weight_block),
+        ("node", "local"),
+        split_axis=0,
+        concat_axis=0,
+        tiled=True,
+    )
     return combine_rows(returned, slot_index, pair_weights)
+
+
+def fused_kernel(
+    nodes, locals_, cap, chunk,
+    ids_ref, wts_ref, hid_ref, w_hbm, out_ref,
+    hot, xs, xr, mix, mixr, wv, outb, zb, pb, rb,
+    w_sem, xsend, xrecv, asend, arecv, zsend, zrecv, psend, precv,
+):
+    half = nodes // 2
+    me_n = lax.axis_index("node")
+    me_l = lax.axis_index("local")
+    me_y, me_c = me_n // 2, me_n % 2
+    rows, width = out_ref.shape
+    pairs = ids_ref.shape[1]
+    picks = pairs // rows
+    slots = nodes * locals_ * cap
+    chunks = width // chunk
+
+    def node_to(d):
+        return ((me_y + d // 2) % half) * 2 + (me_c + d % 2) % 2
+
+    def node_from(d):
+        return ((me_y - d // 2 + half) % half) * 2 + (me_c - d % 2 + 2) % 2
+
+    def local_to(d):
+        return (me_l + d) % locals_
+
+    barrier = pltpu.get_barrier_semaphore()
+    for d in range(nodes):
+        for dl in range(locals_):
+            if d or dl:
+                pl.semaphore_signal(
+                    barrier, inc=1, device_id={"node": node_to(d), "local": local_to(dl)},
+                    device_id_type=MESH,
+                )
+
+    weight_copy = pltpu.make_async_copy(w_hbm.at[0], wv, w_sem)
+    weight_copy.start()
+
+    ids = ids_ref[...]
+    experts = nodes * locals_
+    mine = lax.broadcasted_iota(jnp.int32, (experts, pairs), 0) == ids
+    mine_f = jnp.where(mine, 1.0, 0.0)
+    before = lax.broadcasted_iota(jnp.int32, (pairs, pairs), 0) < lax.broadcasted_iota(
+        jnp.int32, (pairs, pairs), 1
+    )
+    running = jnp.dot(
+        mine_f.astype(BF16), jnp.where(before, 1.0, 0.0).astype(BF16), preferred_element_type=F32
+    )
+    place = jnp.sum(mine_f * running, axis=0, keepdims=True).astype(jnp.int32)
+    slot = ids * cap + place
+    hot[...] = jnp.where(
+        lax.broadcasted_iota(jnp.int32, (slots, pairs), 0) == slot, 1.0, 0.0
+    ).astype(BF16)
+    xs[...] = (
+        jnp.dot(hot[...], hid_ref[...], preferred_element_type=F32).astype(BF16).reshape(xs.shape)
+    )
+    row_of = lax.broadcasted_iota(jnp.int32, (rows, pairs), 1) // picks
+    spread = jnp.where(
+        row_of == lax.broadcasted_iota(jnp.int32, (rows, pairs), 0), wts_ref[...], 0.0
+    ).astype(BF16)
+    mix_all = lax.dot_general(
+        spread, hot[...], (((1,), (1,)), ((), ())), preferred_element_type=F32
+    ).astype(BF16)
+    span = nodes * cap
+    for l in range(locals_):
+        mix[l] = mix_all[:, l * span:(l + 1) * span]
+
+    pl.semaphore_wait(barrier, nodes * locals_ - 1)
+
+    order = list(range(nodes - 1, -1, -1))
+    order = [d for d in order if d >= 2] + [d for d in order if d < 2]
+
+    def hidden_copy(d, dl):
+        n_t, l_t = node_to(d), local_to(dl)
+        return pltpu.make_async_remote_copy(
+            src_ref=xs.at[l_t * nodes + n_t], dst_ref=xr.at[d, me_l],
+            send_sem=xsend.at[d, dl], recv_sem=xrecv.at[d, dl],
+            device_id={"node": n_t, "local": l_t}, device_id_type=MESH,
+        )
+
+    def mix_copy(dl):
+        l_t = local_to(dl)
+        return pltpu.make_async_remote_copy(
+            src_ref=mix.at[l_t], dst_ref=mixr.at[me_l],
+            send_sem=asend.at[dl], recv_sem=arecv.at[dl],
+            device_id={"node": me_n, "local": l_t}, device_id_type=MESH,
+        )
+
+    for d in order:
+        for dl in range(locals_ - 1, -1, -1):
+            if d or dl:
+                hidden_copy(d, dl).start()
+    for dl in range(1, locals_):
+        mix_copy(dl).start()
+    xr[0, me_l] = xs[me_l * nodes + me_n]
+    mixr[me_l] = mix[me_l]
+    weight_copy.wait()
+
+    def return_copy(c, d):
+        return pltpu.make_async_remote_copy(
+            src_ref=outb.at[c, d],
+            dst_ref=zb.at[c, :, pl.ds(pl.multiple_of(me_n * cap, cap), cap), :],
+            send_sem=zsend.at[c, d], recv_sem=zrecv.at[c, d],
+            device_id={"node": node_from(d), "local": me_l}, device_id_type=MESH,
+        )
+
+    def sum_copy(c, dl):
+        l_t = local_to(dl)
+        return pltpu.make_async_remote_copy(
+            src_ref=pb.at[c, l_t], dst_ref=rb.at[c, me_l],
+            send_sem=psend.at[c, dl], recv_sem=precv.at[c, dl],
+            device_id={"node": me_n, "local": l_t}, device_id_type=MESH,
+        )
+
+    for low in list(range(2, nodes, 2)) + [0]:
+        for d in (low, low + 1):
+            for dl in range(locals_):
+                if d or dl:
+                    hidden_copy(d, dl).wait_recv()
+
+        def apply_chunk(c, carry, low=low):
+            cols = pl.ds(pl.multiple_of(c * chunk, chunk), chunk)
+            x = xr[low:low + 2].reshape(2 * locals_ * cap, xr.shape[-1])
+            o = jnp.dot(x, wv[:, cols], preferred_element_type=F32).astype(BF16)
+            o = o.reshape(2, locals_, cap, chunk)
+            for k in range(2):
+                if low + k:
+                    outb[c, low + k] = o[k]
+                    return_copy(c, low + k).start()
+                else:
+                    zb[c, :, pl.ds(pl.multiple_of(me_n * cap, cap), cap), :] = o[k]
+            return carry
+
+        lax.fori_loop(0, chunks, apply_chunk, 0)
+
+    for dl in range(1, locals_):
+        mix_copy(dl).wait_recv()
+
+    def combine_chunk(c, carry):
+        for d in range(1, nodes):
+            return_copy(c, d).wait_recv()
+        for l in range(locals_):
+            pb[c, l] = jnp.dot(mixr[l], zb[c, l], preferred_element_type=F32).astype(BF16)
+        for dl in range(locals_ - 1, 0, -1):
+            sum_copy(c, dl).start()
+        rb[c, me_l] = pb[c, me_l]
+        return carry
+
+    lax.fori_loop(0, chunks, combine_chunk, 0)
+
+    def final_chunk(c, carry):
+        cols = pl.ds(pl.multiple_of(c * chunk, chunk), chunk)
+        for dl in range(1, locals_):
+            sum_copy(c, dl).wait_recv()
+        total = rb[c, 0].astype(F32)
+        for l in range(1, locals_):
+            total = total + rb[c, l].astype(F32)
+        out_ref[:, cols] = total.astype(BF16)
+        return carry
+
+    lax.fori_loop(0, chunks, final_chunk, 0)
+
+    for d in range(nodes):
+        for dl in range(locals_):
+            if d or dl:
+                hidden_copy(d, dl).wait_send()
+    for dl in range(1, locals_):
+        mix_copy(dl).wait_send()
+
+    def drain(c, carry):
+        for d in range(1, nodes):
+            return_copy(c, d).wait_send()
+        for dl in range(1, locals_):
+            sum_copy(c, dl).wait_send()
+        return carry
+
+    lax.fori_loop(0, chunks, drain, 0)
+
+
+def dense_plan(hidden, route_weights, node_groups, group_picks, down_weight, capacity):
+    row_count, pick_count, hidden_width = hidden.shape
+    group_count = node_groups.shape[1]
+    pair_count = pick_count // group_count
+    nodes = lax.axis_size("node")
+    locals_ = lax.axis_size("local")
+    width = down_weight.shape[2]
+    pairs = row_count * pick_count
+    chunk = 512 if width % 512 == 0 else 128
+    chunks = width // chunk
+    ids = group_picks * nodes + jnp.repeat(node_groups, pair_count, axis=1)
+    dma = pltpu.SemaphoreType.DMA
+    vmem = pl.BlockSpec(memory_space=pltpu.VMEM)
+    return pl.pallas_call(
+        functools.partial(fused_kernel, nodes, locals_, capacity, chunk),
+        out_shape=jax.ShapeDtypeStruct((row_count, width), BF16),
+        in_specs=[vmem, vmem, vmem, pl.BlockSpec(memory_space=pl.ANY)],
+        out_specs=vmem,
+        scratch_shapes=[
+            pltpu.VMEM((nodes * locals_ * capacity, pairs), BF16),
+            pltpu.VMEM((nodes * locals_, capacity, hidden_width), BF16),
+            pltpu.VMEM((nodes, locals_, capacity, hidden_width), BF16),
+            pltpu.VMEM((locals_, row_count, nodes * capacity), BF16),
+            pltpu.VMEM((locals_, row_count, nodes * capacity), BF16),
+            pltpu.VMEM((hidden_width, width), BF16),
+            pltpu.VMEM((chunks, nodes, locals_, capacity, chunk), BF16),
+            pltpu.VMEM((chunks, locals_, nodes * capacity, chunk), BF16),
+            pltpu.VMEM((chunks, locals_, row_count, chunk), BF16),
+            pltpu.VMEM((chunks, locals_, row_count, chunk), BF16),
+            dma,
+            dma((nodes, locals_)),
+            dma((nodes, locals_)),
+            dma((locals_,)),
+            dma((locals_,)),
+            dma((chunks, nodes)),
+            dma((chunks, nodes)),
+            dma((chunks, locals_)),
+            dma((chunks, locals_)),
+        ],
+        compiler_params=pltpu.CompilerParams(
+            collective_id=0, has_side_effects=True, vmem_limit_bytes=56 * 1024 * 1024
+        ),
+    )(
+        ids.reshape(1, pairs),
+        route_weights.astype(F32).reshape(1, pairs),
+        hidden.reshape(pairs, hidden_width),
+        down_weight,
+    )
+
+
+def shards(hidden, gates, node_groups, group_picks, down_weight):
+    row_count = hidden.shape[0]
+    nodes = lax.axis_size("node")
+    capacity = 2 * row_count // lax.axis_size("local")
+    route_weights = (route_scale * gates / jnp.sum(gates, axis=1, keepdims=True)).astype(BF16)
+    if nodes == node_groups.shape[1] and nodes % 2 == 0:
+        return dense_plan(hidden, route_weights, node_groups, group_picks, down_weight, capacity)
+    return sparse_plan(
+        hidden, route_weights, node_groups, group_picks, down_weight[0], capacity
+    )
 
 
 def solution(mesh):

time: 172 us -> 85.6 us (0.50)
  waiting for transfers between devices: 82.8 us -> 0 us
  Pallas kernels: 0 us -> 79.2 us
  blocking collectives: 34.2 us -> 0 us
  local copies, waits for them, and re-layouts: 23.9 us -> 4.02 us
  other arithmetic: 17.1 us -> 2.08 us
  matrix products: 8.55 us -> 0 us
  starting transfers between devices: 4.81 us -> 0 us
    all_to_all x1 -> x0, waiting for transfers between devices: 82.8 us -> none  [shards(): lax.all_to_all(expert_apply(lax.all_to_all(outgoing.reshape(device_count,...]
    pallas_call x0 -> x1, Pallas kernels: none -> 79.2 us  [dense_plan(): pl.pallas_call(functools.partial(fused_kernel, nodes, locals_, capacity,...]
    all_to_all x1 -> x0, blocking collectives: 34.2 us -> none  [shards(): lax.all_to_all(outgoing.reshape(device_count, capacity, hidden_width), ('...]
    reduce_sum x3 -> x0, other arithmetic: 15.1 us -> none  [the longest x1 11.7 us: combine_rows(): jnp.sum(pair_weights.astype(jnp.float32)[..., None] * picked, axis=2)]
    gather x1 -> x0, local copies, waits for them, and re-layouts: 10.4 us -> none  [combine_rows(): picked = returned.reshape(-1, model_width)[slot_index].astype(jnp.float32)]
    convert_element_type x2 -> x0, local copies, waits for them, and re-layouts: 8.75 us -> none  [the longest x1 8.61 us: combine_rows(): picked = returned.reshape(-1, model_width)[slot_index].astype(jnp.float32)]
    dot_general x1 -> x0, matrix products: 8.55 us -> none  [expert_apply(): jnp.dot(flat_rows, weight_block, preferred_element_type=jnp.float32)]
    all_to_all x1 -> x0, starting transfers between devices: 4.81 us -> none  [shards(): lax.all_to_all(expert_apply(lax.all_to_all(outgoing.reshape(device_count,...]
  transfers between devices with their start and end apart: 1 -> 0, of which waited for: 1 -> 0; matrix products, arithmetic and copies ran while one was open for 0% -> 0% of each run, Pallas kernels for 0% -> 0%
where the time goes in v1:
time: 85.6 us; the launch traced here: 85.3 us
  Pallas kernels  79.2 us (93%)
  local copies, waits for them, and re-layouts  4.02 us (5%)
  other arithmetic  2.08 us (2%)
    pallas_call x1, Pallas kernels, dense_plan(): pl.pallas_call(functools.partial(fused_kernel, nodes, locals_, capacity,...  79.2 us
    unnamed x1, local copies, waits for them, and re-layouts  1.82 us

profile of v1, /device:TPU:0, one launch (start us, length us, event | category | flops | bytes accessed | tf_op | source)
XLA Modules:
  0.0 85.3 jit_solution(10395050332332485973)
XLA Ops:
  0.0 0.7 reduce_sum.9
  0.7 0.7 fusion
  1.4 0.7 broadcast_in_dim.4
  2.1 0.7 multiply_add_fusion
  2.8 0.1 copy.8
  2.9 0.7 reshape.16.ids_ref
  3.5 0.1 copy.9
  3.6 0.7 reshape.21.wts_ref
  4.3 79.2 %shard_map.55 = bf16[64,3584]{1,0:T(8,128)(2,1)} custom-call(s32[1,512]{1,0:T(1,128)} %reshape.16.ids_ref, f32[1,512]{1,0:T(1,128)} %reshape.21.wts_ref, bf16[512,1024]{1,0:T(8,128)(2,1)} %bitcast.2, bf16[1,1024,3584]{2,1,0:T(8,128)(2,1)} %w_hbm.1), custom_call_target="tpu_custom_call" | custom-call | tf_op jit(solution)/shard_map/pallas_call | solution.py:270
  83.5 1.8 %copy.11 = bf16[64,3584]{1,0:T(8,128)(2,1)} copy(bf16[64,3584]{1,0:T(8,128)(2,1)} %shard_map.55) | data formatting | bytes 917504

commit v2 on v1

--- a/solution.py
+++ b/solution.py
@@ -79,7 +79,7 @@
 def fused_kernel(
     nodes, locals_, cap, chunk,
     ids_ref, wts_ref, hid_ref, w_hbm, out_ref,
-    hot, xs, xr, mix, mixr, wv, outb, zb, pb, rb,
+    hot, xs, xr, mix, mixr, wv, outb, zb, pb, mb, rb,
     w_sem, xsend, xrecv, asend, arecv, zsend, zrecv, psend, precv,
 ):
     half = nodes // 2
@@ -181,12 +181,31 @@
             device_id={"node": node_from(d), "local": me_l}, device_id_type=MESH,
         )
 
-    def sum_copy(c, dl):
-        l_t = local_to(dl)
-        return pltpu.make_async_remote_copy(
-            src_ref=pb.at[c, l_t], dst_ref=rb.at[c, me_l],
-            send_sem=psend.at[c, dl], recv_sem=precv.at[c, dl],
-            device_id={"node": me_n, "local": l_t}, device_id_type=MESH,
+    side = me_l // 2
+    mate = me_l + 1 - 2 * (me_l % 2)
+    inner = me_l == 1 + side
+    edge = me_l != 1 + side
+    away = (1 - side) * 2
+
+    def mate_copy(c):
+        return pltpu.make_async_remote_copy(
+            src_ref=pb.at[c, mate], dst_ref=rb.at[c, 0],
+            send_sem=psend.at[c, 0], recv_sem=precv.at[c, 0],
+            device_id={"node": me_n, "local": mate}, device_id_type=MESH,
+        )
+
+    def forward_copy(c):
+        return pltpu.make_async_remote_copy(
+            src_ref=pb.at[c, pl.ds(away, 2)], dst_ref=mb.at[c],
+            send_sem=psend.at[c, 1], recv_sem=precv.at[c, 1],
+            device_id={"node": me_n, "local": mate}, device_id_type=MESH,
+        )
+
+    def cross_copy(c, t):
+        return pltpu.make_async_remote_copy(
+            src_ref=mb.at[c, t], dst_ref=rb.at[c, 1],
+            send_sem=psend.at[c, 2 + t], recv_sem=precv.at[c, 2],
+            device_id={"node": me_n, "local": away + t}, device_id_type=MESH,
         )
 
     for low in list(range(2, nodes, 2)) + [0]:
@@ -213,25 +232,40 @@
     for dl in range(1, locals_):
         mix_copy(dl).wait_recv()
 
-    def combine_chunk(c, carry):
+    def combine(c):
         for d in range(1, nodes):
             return_copy(c, d).wait_recv()
         for l in range(locals_):
             pb[c, l] = jnp.dot(mixr[l], zb[c, l], preferred_element_type=F32).astype(BF16)
-        for dl in range(locals_ - 1, 0, -1):
-            sum_copy(c, dl).start()
-        rb[c, me_l] = pb[c, me_l]
+
+        @pl.when(edge)
+        def _():
+            forward_copy(c).start()
+
+        mate_copy(c).start()
+
+    def merge(c):
+        @pl.when(inner)
+        def _():
+            forward_copy(c).wait_recv()
+            for t in range(2):
+                mb[c, t] = (mb[c, t].astype(F32) + pb[c, away + t].astype(F32)).astype(BF16)
+                cross_copy(c, t).start()
+
+    def combine_chunk(c, carry):
+        combine(c)
+        merge(c - 1)
         return carry
 
-    lax.fori_loop(0, chunks, combine_chunk, 0)
+    combine(0)
+    lax.fori_loop(1, chunks, combine_chunk, 0)
+    merge(chunks - 1)
 
     def final_chunk(c, carry):
         cols = pl.ds(pl.multiple_of(c * chunk, chunk), chunk)
-        for dl in range(1, locals_):
-            sum_copy(c, dl).wait_recv()
-        total = rb[c, 0].astype(F32)
-        for l in range(1, locals_):
-            total = total + rb[c, l].astype(F32)
+        mate_copy(c).wait_recv()
+        cross_copy(c, 0).wait_recv()
+        total = pb[c, me_l].astype(F32) + rb[c, 0].astype(F32) + rb[c, 1].astype(F32)
         out_ref[:, cols] = total.astype(BF16)
         return carry
 
@@ -247,8 +281,17 @@
     def drain(c, carry):
         for d in range(1, nodes):
             return_copy(c, d).wait_send()
-        for dl in range(1, locals_):
-            sum_copy(c, dl).wait_send()
+        mate_copy(c).wait_send()
+
+        @pl.when(edge)
+        def _():
+            forward_copy(c).wait_send()
+
+        @pl.when(inner)
+        def _():
+            for t in range(2):
+                cross_copy(c, t).wait_send()
+
         return carry
 
     lax.fori_loop(0, chunks, drain, 0)
@@ -282,7 +325,8 @@
             pltpu.VMEM((chunks, nodes, locals_, capacity, chunk), BF16),
             pltpu.VMEM((chunks, locals_, nodes * capacity, chunk), BF16),
             pltpu.VMEM((chunks, locals_, row_count, chunk), BF16),
-            pltpu.VMEM((chunks, locals_, row_count, chunk), BF16),
+            pltpu.VMEM((chunks, 2, row_count, chunk), BF16),
+            pltpu.VMEM((chunks, 2, row_count, chunk), BF16),
             dma,
             dma((nodes, locals_)),
             dma((nodes, locals_)),
@@ -290,8 +334,8 @@
             dma((locals_,)),
             dma((chunks, nodes)),
             dma((chunks, nodes)),
-            dma((chunks, locals_)),
-            dma((chunks, locals_)),
+            dma((chunks, 4)),
+            dma((chunks, 3)),
         ],
         compiler_params=pltpu.CompilerParams(
             collective_id=0, has_side_effects=True, vmem_limit_bytes=56 * 1024 * 1024
@@ -309,7 +353,7 @@
     nodes = lax.axis_size("node")
     capacity = 2 * row_count // lax.axis_size("local")
     route_weights = (route_scale * gates / jnp.sum(gates, axis=1, keepdims=True)).astype(BF16)
-    if nodes == node_groups.shape[1] and nodes % 2 == 0:
+    if nodes == node_groups.shape[1] and nodes % 2 == 0 and lax.axis_size("local") == 4:
         return dense_plan(hidden, route_weights, node_groups, group_picks, down_weight, capacity)
     return sparse_plan(
         hidden, route_weights, node_groups, group_picks, down_weight[0], capacity

time: 85.6 us -> 81.2 us (0.949)
  the two profiles are of different devices: /device:TPU:0 before, /device:TPU:25 now
where the time goes in v2:
time: 81.2 us; the launch traced here: 80.9 us
  Pallas kernels  74.8 us (92%)
  local copies, waits for them, and re-layouts  4.02 us (5%)
  other arithmetic  2.08 us (3%)
    pallas_call x1, Pallas kernels, dense_plan(): pl.pallas_call(functools.partial(fused_kernel, nodes, locals_, capacity,...  74.8 us
    unnamed x1, local copies, waits for them, and re-layouts  1.82 us

profile of v2, /device:TPU:25, one launch (start us, length us, event | category | flops | bytes accessed | tf_op | source)
XLA Modules:
  0.0 80.9 jit_solution(15934773854100517188)
XLA Ops:
  0.0 0.7 reduce_sum.9
  0.7 0.7 fusion
  1.4 0.7 broadcast_in_dim.4
  2.1 0.7 multiply_add_fusion
  2.8 0.1 copy.8
  2.9 0.7 reshape.16.ids_ref
  3.5 0.1 copy.9
  3.6 0.7 reshape.21.wts_ref
  4.3 74.8 %shard_map.55 = bf16[64,3584]{1,0:T(8,128)(2,1)} custom-call(s32[1,512]{1,0:T(1,128)} %reshape.16.ids_ref, f32[1,512]{1,0:T(1,128)} %reshape.21.wts_ref, bf16[512,1024]{1,0:T(8,128)(2,1)} %bitcast.2, bf16[1,1024,3584]{2,1,0:T(8,128)(2,1)} %w_hbm.1), custom_call_target="tpu_custom_call" | custom-call | tf_op jit(solution)/shard_map/pallas_call | solution.py:313
  79.1 1.8 %copy.11 = bf16[64,3584]{1,0:T(8,128)(2,1)} copy(bf16[64,3584]{1,0:T(8,128)(2,1)} %shard_map.55) | data formatting | bytes 917504

commit v3 on v2

--- a/solution.py
+++ b/solution.py
@@ -144,16 +144,29 @@
 
     pl.semaphore_wait(barrier, nodes * locals_ - 1)
 
-    order = list(range(nodes - 1, -1, -1))
-    order = [d for d in order if d >= 2] + [d for d in order if d < 2]
-
-    def hidden_copy(d, dl):
-        n_t, l_t = node_to(d), local_to(dl)
+    side = me_l // 2
+    mate = me_l + 1 - 2 * (me_l % 2)
+    inner = me_l == 1 + side
+    edge = me_l != 1 + side
+    away = (1 - side) * 2
+
+    def place_of(q):
+        return (me_l, mate, away, away + 1)[q]
+
+    def hidden_copy(d, q):
+        n_t, l_t = node_to(d), place_of(q)
         return pltpu.make_async_remote_copy(
             src_ref=xs.at[l_t * nodes + n_t], dst_ref=xr.at[d, me_l],
-            send_sem=xsend.at[d, dl], recv_sem=xrecv.at[d, dl],
+            send_sem=xsend.at[d, q], recv_sem=xrecv.at[d, me_l],
             device_id={"node": n_t, "local": l_t}, device_id_type=MESH,
         )
+
+    def hidden_wait(d, l):
+        pltpu.make_async_remote_copy(
+            src_ref=xs.at[0], dst_ref=xr.at[d, l],
+            send_sem=xsend.at[d, 0], recv_sem=xrecv.at[d, l],
+            device_id={"node": me_n, "local": me_l}, device_id_type=MESH,
+        ).wait_recv()
 
     def mix_copy(dl):
         l_t = local_to(dl)
@@ -163,29 +176,30 @@
             device_id={"node": me_n, "local": l_t}, device_id_type=MESH,
         )
 
-    for d in order:
-        for dl in range(locals_ - 1, -1, -1):
-            if d or dl:
-                hidden_copy(d, dl).start()
+    cross_nodes = list(range(2, nodes))
+    for ds, qs in ((cross_nodes, (0, 1)), (cross_nodes, (2, 3)), ((1, 0), (2, 3, 1, 0))):
+        for q in qs:
+            for d in ds:
+                if d or q:
+                    hidden_copy(d, q).start()
     for dl in range(1, locals_):
         mix_copy(dl).start()
     xr[0, me_l] = xs[me_l * nodes + me_n]
     mixr[me_l] = mix[me_l]
     weight_copy.wait()
 
-    def return_copy(c, d):
-        return pltpu.make_async_remote_copy(
-            src_ref=outb.at[c, d],
-            dst_ref=zb.at[c, :, pl.ds(pl.multiple_of(me_n * cap, cap), cap), :],
-            send_sem=zsend.at[c, d], recv_sem=zrecv.at[c, d],
+    def half_of(h):
+        return pl.ds(side * 2 if h == 0 else away, 2)
+
+    my_slots = pl.ds(pl.multiple_of(me_n * cap, cap), cap)
+
+    def return_copy(c, d, h):
+        return pltpu.make_async_remote_copy(
+            src_ref=outb.at[c, d, half_of(h)],
+            dst_ref=zb.at[c, half_of(h), my_slots, :],
+            send_sem=zsend.at[c, d, h], recv_sem=zrecv.at[c, d, h],
             device_id={"node": node_from(d), "local": me_l}, device_id_type=MESH,
         )
-
-    side = me_l // 2
-    mate = me_l + 1 - 2 * (me_l % 2)
-    inner = me_l == 1 + side
-    edge = me_l != 1 + side
-    away = (1 - side) * 2
 
     def mate_copy(c):
         return pltpu.make_async_remote_copy(
@@ -208,41 +222,62 @@
             device_id={"node": me_n, "local": away + t}, device_id_type=MESH,
         )
 
-    for low in list(range(2, nodes, 2)) + [0]:
-        for d in (low, low + 1):
-            for dl in range(locals_):
-                if d or dl:
-                    hidden_copy(d, dl).wait_recv()
-
-        def apply_chunk(c, carry, low=low):
+    for h in range(2):
+        for d in cross_nodes:
+            for t in range(2):
+                hidden_wait(d, half_of(h).start + t)
+
+        def cross_chunk(c, carry, h=h):
             cols = pl.ds(pl.multiple_of(c * chunk, chunk), chunk)
-            x = xr[low:low + 2].reshape(2 * locals_ * cap, xr.shape[-1])
+            x = xr[2:nodes, half_of(h)].reshape((nodes - 2) * 2 * cap, xr.shape[-1])
             o = jnp.dot(x, wv[:, cols], preferred_element_type=F32).astype(BF16)
-            o = o.reshape(2, locals_, cap, chunk)
-            for k in range(2):
-                if low + k:
-                    outb[c, low + k] = o[k]
-                    return_copy(c, low + k).start()
-                else:
-                    zb[c, :, pl.ds(pl.multiple_of(me_n * cap, cap), cap), :] = o[k]
+            o = o.reshape(nodes - 2, 2, cap, chunk)
+            for d in cross_nodes:
+                outb[c, d, half_of(h)] = o[d - 2]
+                return_copy(c, d, h).start()
             return carry
 
-        lax.fori_loop(0, chunks, apply_chunk, 0)
+        lax.fori_loop(0, chunks, cross_chunk, 0)
+
+    for q in range(4):
+        hidden_wait(1, place_of(q))
+        if q:
+            hidden_wait(0, place_of(q))
+
+    def near_chunk(c, carry):
+        cols = pl.ds(pl.multiple_of(c * chunk, chunk), chunk)
+        x = xr[0:2].reshape(2 * locals_ * cap, xr.shape[-1])
+        o = jnp.dot(x, wv[:, cols], preferred_element_type=F32).astype(BF16)
+        o = o.reshape(2, locals_, cap, chunk)
+        outb[c, 1] = o[1]
+        for h in range(2):
+            return_copy(c, 1, h).start()
+        zb[c, :, my_slots, :] = o[0]
+        return carry
+
+    lax.fori_loop(0, chunks, near_chunk, 0)
 
     for dl in range(1, locals_):
         mix_copy(dl).wait_recv()
 
-    def combine(c):
+    def combine(c, h):
         for d in range(1, nodes):
-            return_copy(c, d).wait_recv()
-        for l in range(locals_):
+            return_copy(c, d, h).wait_recv()
+        for t in range(2):
+            l = half_of(h).start + t
             pb[c, l] = jnp.dot(mixr[l], zb[c, l], preferred_element_type=F32).astype(BF16)
+
+    def combine_own(c, carry):
+        combine(c, 0)
+        mate_copy(c).start()
+        return carry
+
+    def combine_away(c):
+        combine(c, 1)
 
         @pl.when(edge)
         def _():
             forward_copy(c).start()
-
-        mate_copy(c).start()
 
     def merge(c):
         @pl.when(inner)
@@ -253,11 +288,12 @@
                 cross_copy(c, t).start()
 
     def combine_chunk(c, carry):
-        combine(c)
+        combine_away(c)
         merge(c - 1)
         return carry
 
-    combine(0)
+    lax.fori_loop(0, chunks, combine_own, 0)
+    combine_away(0)
     lax.fori_loop(1, chunks, combine_chunk, 0)
     merge(chunks - 1)
 
@@ -272,15 +308,16 @@
     lax.fori_loop(0, chunks, final_chunk, 0)
 
     for d in range(nodes):
-        for dl in range(locals_):
-            if d or dl:
-                hidden_copy(d, dl).wait_send()
+        for q in range(4):
+            if d or q:
+                hidden_copy(d, q).wait_send()
     for dl in range(1, locals_):
         mix_copy(dl).wait_send()
 
     def drain(c, carry):
         for d in range(1, nodes):
-            return_copy(c, d).wait_send()
+            for h in range(2):
+                return_copy(c, d, h).wait_send()
         mate_copy(c).wait_send()
 
         @pl.when(edge)
@@ -332,8 +369,8 @@
             dma((nodes, locals_)),
             dma((locals_,)),
             dma((locals_,)),
-            dma((chunks, nodes)),
-            dma((chunks, nodes)),
+            dma((chunks, nodes, 2)),
+            dma((chunks, nodes, 2)),
             dma((chunks, 4)),
             dma((chunks, 3)),
         ],

time: 81.2 us -> 82.4 us (1.015)
  the two profiles are of different devices: /device:TPU:25 before, /device:TPU:0 now
where the time goes in v3:
time: 82.4 us; the launch traced here: 82.1 us
  Pallas kernels  76 us (92%)
  local copies, waits for them, and re-layouts  4.02 us (5%)
  other arithmetic  2.08 us (3%)
    pallas_call x1, Pallas kernels, dense_plan(): pl.pallas_call(functools.partial(fused_kernel, nodes, locals_, capacity,...  76 us
    unnamed x1, local copies, waits for them, and re-layouts  1.82 us

profile of v3, /device:TPU:0, one launch (start us, length us, event | category | flops | bytes accessed | tf_op | source)
XLA Modules:
  0.0 82.1 jit_solution(15874434594979556746)
XLA Ops:
  0.0 0.7 reduce_sum.9
  0.7 0.7 fusion
  1.4 0.7 broadcast_in_dim.4
  2.1 0.7 multiply_add_fusion
  2.8 0.1 copy.8
  2.9 0.7 reshape.16.ids_ref
  3.5 0.1 copy.9
  3.6 0.7 reshape.21.wts_ref
  4.3 76.0 %shard_map.55 = bf16[64,3584]{1,0:T(8,128)(2,1)} custom-call(s32[1,512]{1,0:T(1,128)} %reshape.16.ids_ref, f32[1,512]{1,0:T(1,128)} %reshape.21.wts_ref, bf16[512,1024]{1,0:T(8,128)(2,1)} %bitcast.2, bf16[1,1024,3584]{2,1,0:T(8,128)(2,1)} %w_hbm.1), custom_call_target="tpu_custom_call" | custom-call | tf_op jit(solution)/shard_map/pallas_call | solution.py:350
  80.3 1.8 %copy.11 = bf16[64,3584]{1,0:T(8,128)(2,1)} copy(bf16[64,3584]{1,0:T(8,128)(2,1)} %shard_map.55) | data formatting | bytes 917504

commit v4 on v2

--- a/solution.py
+++ b/solution.py
@@ -78,7 +78,7 @@
 
 def fused_kernel(
     nodes, locals_, cap, chunk,
-    ids_ref, wts_ref, hid_ref, w_hbm, out_ref,
+    gates_ref, groups_ref, picks_ref, hid_ref, w_hbm, out_ref,
     hot, xs, xr, mix, mixr, wv, outb, zb, pb, mb, rb,
     w_sem, xsend, xrecv, asend, arecv, zsend, zrecv, psend, precv,
 ):
@@ -87,8 +87,8 @@
     me_l = lax.axis_index("local")
     me_y, me_c = me_n // 2, me_n % 2
     rows, width = out_ref.shape
-    pairs = ids_ref.shape[1]
-    picks = pairs // rows
+    picks, pairs = gates_ref.shape[0], hid_ref.shape[0]
+    share = picks // groups_ref.shape[0]
     slots = nodes * locals_ * cap
     chunks = width // chunk
 
@@ -113,7 +113,25 @@
     weight_copy = pltpu.make_async_copy(w_hbm.at[0], wv, w_sem)
     weight_copy.start()
 
-    ids = ids_ref[...]
+    gates = gates_ref[...]
+    weights = route_scale * gates / jnp.sum(gates, axis=0, keepdims=True)
+    groups = jnp.concatenate(
+        [groups_ref[j // share:j // share + 1, :] for j in range(picks)], axis=0
+    )
+    numbers = (picks_ref[...] * nodes + groups).astype(F32)
+    lay = lax.broadcasted_iota(jnp.int32, (rows, pairs), 1) // picks == lax.broadcasted_iota(
+        jnp.int32, (rows, pairs), 0
+    )
+    tables = jnp.dot(
+        jnp.concatenate([weights, numbers], axis=0).astype(BF16),
+        jnp.where(lay, 1.0, 0.0).astype(BF16),
+        preferred_element_type=F32,
+    )
+    own = lax.broadcasted_iota(jnp.int32, (picks, pairs), 1) % picks == lax.broadcasted_iota(
+        jnp.int32, (picks, pairs), 0
+    )
+    wts = jnp.sum(jnp.where(own, tables[:picks], 0.0), axis=0, keepdims=True)
+    ids = jnp.sum(jnp.where(own, tables[picks:], 0.0), axis=0, keepdims=True).astype(jnp.int32)
     experts = nodes * locals_
     mine = lax.broadcasted_iota(jnp.int32, (experts, pairs), 0) == ids
     mine_f = jnp.where(mine, 1.0, 0.0)
@@ -131,10 +149,7 @@
     xs[...] = (
         jnp.dot(hot[...], hid_ref[...], preferred_element_type=F32).astype(BF16).reshape(xs.shape)
     )
-    row_of = lax.broadcasted_iota(jnp.int32, (rows, pairs), 1) // picks
-    spread = jnp.where(
-        row_of == lax.broadcasted_iota(jnp.int32, (rows, pairs), 0), wts_ref[...], 0.0
-    ).astype(BF16)
+    spread = jnp.where(lay, wts, 0.0).astype(BF16)
     mix_all = lax.dot_general(
         spread, hot[...], (((1,), (1,)), ((), ())), preferred_element_type=F32
     ).astype(BF16)
@@ -208,26 +223,35 @@
             device_id={"node": me_n, "local": away + t}, device_id_type=MESH,
         )
 
-    for low in list(range(2, nodes, 2)) + [0]:
+    lows = list(range(2, nodes, 2)) + [0]
+
+    def hidden_wait(low):
         for d in (low, low + 1):
             for dl in range(locals_):
                 if d or dl:
                     hidden_copy(d, dl).wait_recv()
 
-        def apply_chunk(c, carry, low=low):
-            cols = pl.ds(pl.multiple_of(c * chunk, chunk), chunk)
-            x = xr[low:low + 2].reshape(2 * locals_ * cap, xr.shape[-1])
-            o = jnp.dot(x, wv[:, cols], preferred_element_type=F32).astype(BF16)
-            o = o.reshape(2, locals_, cap, chunk)
-            for k in range(2):
-                if low + k:
-                    outb[c, low + k] = o[k]
-                    return_copy(c, low + k).start()
-                else:
-                    zb[c, :, pl.ds(pl.multiple_of(me_n * cap, cap), cap), :] = o[k]
+    def apply(c, low):
+        cols = pl.ds(pl.multiple_of(c * chunk, chunk), chunk)
+        x = xr[low:low + 2].reshape(2 * locals_ * cap, xr.shape[-1])
+        o = jnp.dot(x, wv[:, cols], preferred_element_type=F32).astype(BF16)
+        o = o.reshape(2, locals_, cap, chunk)
+        for k in range(2):
+            if low + k:
+                outb[c, low + k] = o[k]
+                return_copy(c, low + k).start()
+            else:
+                zb[c, :, pl.ds(pl.multiple_of(me_n * cap, cap), cap), :] = o[k]
+
+    ahead = min(5, chunks)
+    for low in lows:
+        hidden_wait(low)
+
+        def early_chunk(c, carry, low=low):
+            apply(c, low)
             return carry
 
-        lax.fori_loop(0, chunks, apply_chunk, 0)
+        lax.fori_loop(0, ahead, early_chunk, 0)
 
     for dl in range(1, locals_):
         mix_copy(dl).wait_recv()
@@ -254,11 +278,19 @@
 
     def combine_chunk(c, carry):
         combine(c)
-        merge(c - 1)
+
+        @pl.when(c + ahead < chunks)
+        def _():
+            for low in lows:
+                apply(c + ahead, low)
+
+        @pl.when(c > 0)
+        def _():
+            merge(c - 1)
+
         return carry
 
-    combine(0)
-    lax.fori_loop(1, chunks, combine_chunk, 0)
+    lax.fori_loop(0, chunks, combine_chunk, 0)
     merge(chunks - 1)
 
     def final_chunk(c, carry):
@@ -297,23 +329,20 @@
     lax.fori_loop(0, chunks, drain, 0)
 
 
-def dense_plan(hidden, route_weights, node_groups, group_picks, down_weight, capacity):
+def dense_plan(hidden, gates, node_groups, group_picks, down_weight, capacity):
     row_count, pick_count, hidden_width = hidden.shape
-    group_count = node_groups.shape[1]
-    pair_count = pick_count // group_count
     nodes = lax.axis_size("node")
     locals_ = lax.axis_size("local")
     width = down_weight.shape[2]
     pairs = row_count * pick_count
-    chunk = 512 if width % 512 == 0 else 128
+    chunk = 256 if width % 256 == 0 else 128
     chunks = width // chunk
-    ids = group_picks * nodes + jnp.repeat(node_groups, pair_count, axis=1)
     dma = pltpu.SemaphoreType.DMA
     vmem = pl.BlockSpec(memory_space=pltpu.VMEM)
     return pl.pallas_call(
         functools.partial(fused_kernel, nodes, locals_, capacity, chunk),
         out_shape=jax.ShapeDtypeStruct((row_count, width), BF16),
-        in_specs=[vmem, vmem, vmem, pl.BlockSpec(memory_space=pl.ANY)],
+        in_specs=[vmem, vmem, vmem, vmem, pl.BlockSpec(memory_space=pl.ANY)],
         out_specs=vmem,
         scratch_shapes=[
             pltpu.VMEM((nodes * locals_ * capacity, pairs), BF16),
@@ -341,8 +370,9 @@
             collective_id=0, has_side_effects=True, vmem_limit_bytes=56 * 1024 * 1024
         ),
     )(
-        ids.reshape(1, pairs),
-        route_weights.astype(F32).reshape(1, pairs),
+        gates.T,
+        node_groups.T,
+        group_picks.T,
         hidden.reshape(pairs, hidden_width),
         down_weight,
     )
@@ -352,9 +382,9 @@
     row_count = hidden.shape[0]
     nodes = lax.axis_size("node")
     capacity = 2 * row_count // lax.axis_size("local")
+    if nodes == node_groups.shape[1] and nodes % 2 == 0 and lax.axis_size("local") == 4:
+        return dense_plan(hidden, gates, node_groups, group_picks, down_weight, capacity)
     route_weights = (route_scale * gates / jnp.sum(gates, axis=1, keepdims=True)).astype(BF16)
-    if nodes == node_groups.shape[1] and nodes % 2 == 0 and lax.axis_size("local") == 4:
-        return dense_plan(hidden, route_weights, node_groups, group_picks, down_weight, capacity)
     return sparse_plan(
         hidden, route_weights, node_groups, group_picks, down_weight[0], capacity
     )

time: 81.2 us -> 75.7 us (0.932)
  the two profiles are of different devices: /device:TPU:25 before, /device:TPU:0 now
where the time goes in v4:
time: 75.7 us; the launch traced here: 74.7 us
  Pallas kernels  72.9 us (96%)
  local copies, waits for them, and re-layouts  1.82 us (2%)
    pallas_call x1, Pallas kernels, dense_plan(): pl.pallas_call(functools.partial(fused_kernel, nodes, locals_, capacity,...  72.9 us
    unnamed x1, local copies, waits for them, and re-layouts  1.82 us

profile of v4, /device:TPU:0, one launch (start us, length us, event | category | flops | bytes accessed | tf_op | source)
XLA Modules:
  0.0 74.7 jit_solution(15912164530918864073)
XLA Ops:
  0.0 72.9 %shard_map.55 = bf16[64,3584]{1,0:T(8,128)(2,1)} custom-call(f32[8,64]{1,0:T(8,128)} %bitcast.5, s32[4,64]{1,0:T(4,128)} %bitcast.7, s32[8,64]{1,0:T(8,128)} %bitcast.6, bf16[512,1024]{1,0:T(8,128)(2,1)} %bitcast.4, bf16[1,1024,3584]{2,1,0:T(8,128)(2,1)} %w_hbm.1), custom_call_target="tpu_custom_call" | custom-call | tf_op jit(solution)/shard_map/pallas_call | solution.py:342
  72.9 1.8 %copy.7 = bf16[64,3584]{1,0:T(8,128)(2,1)} copy(bf16[64,3584]{1,0:T(8,128)(2,1)} %shard_map.55) | data formatting | bytes 917504

commit v5 on v4

--- a/solution.py
+++ b/solution.py
@@ -149,6 +149,33 @@
     xs[...] = (
         jnp.dot(hot[...], hid_ref[...], preferred_element_type=F32).astype(BF16).reshape(xs.shape)
     )
+
+    pl.semaphore_wait(barrier, nodes * locals_ - 1)
+
+    order = list(range(nodes - 1, -1, -1))
+    order = [d for d in order if d >= 2] + [d for d in order if d < 2]
+
+    def hidden_copy(d, dl):
+        n_t, l_t = node_to(d), local_to(dl)
+        return pltpu.make_async_remote_copy(
+            src_ref=xs.at[l_t * nodes + n_t], dst_ref=xr.at[d, me_l],
+            send_sem=xsend.at[d, dl], recv_sem=xrecv.at[d, dl],
+            device_id={"node": n_t, "local": l_t}, device_id_type=MESH,
+        )
+
+    def mix_copy(dl):
+        l_t = local_to(dl)
+        return pltpu.make_async_remote_copy(
+            src_ref=mix.at[l_t], dst_ref=mixr.at[me_l],
+            send_sem=asend.at[dl], recv_sem=arecv.at[dl],
+            device_id={"node": me_n, "local": l_t}, device_id_type=MESH,
+        )
+
+    for d in order:
+        for dl in range(locals_ - 1, -1, -1):
+            if d or dl:
+                hidden_copy(d, dl).start()
+
     spread = jnp.where(lay, wts, 0.0).astype(BF16)
     mix_all = lax.dot_general(
         spread, hot[...], (((1,), (1,)), ((), ())), preferred_element_type=F32
@@ -156,32 +183,6 @@
     span = nodes * cap
     for l in range(locals_):
         mix[l] = mix_all[:, l * span:(l + 1) * span]
-
-    pl.semaphore_wait(barrier, nodes * locals_ - 1)
-
-    order = list(range(nodes - 1, -1, -1))
-    order = [d for d in order if d >= 2] + [d for d in order if d < 2]
-
-    def hidden_copy(d, dl):
-        n_t, l_t = node_to(d), local_to(dl)
-        return pltpu.make_async_remote_copy(
-            src_ref=xs.at[l_t * nodes + n_t], dst_ref=xr.at[d, me_l],
-            send_sem=xsend.at[d, dl], recv_sem=xrecv.at[d, dl],
-            device_id={"node": n_t, "local": l_t}, device_id_type=MESH,
-        )
-
-    def mix_copy(dl):
-        l_t = local_to(dl)
-        return pltpu.make_async_remote_copy(
-            src_ref=mix.at[l_t], dst_ref=mixr.at[me_l],
-            send_sem=asend.at[dl], recv_sem=arecv.at[dl],
-            device_id={"node": me_n, "local": l_t}, device_id_type=MESH,
-        )
-
-    for d in order:
-        for dl in range(locals_ - 1, -1, -1):
-            if d or dl:
-                hidden_copy(d, dl).start()
     for dl in range(1, locals_):
         mix_copy(dl).start()
     xr[0, me_l] = xs[me_l * nodes + me_n]

time: 75.7 us -> 75.8 us (level)
  no operation moved by 1% of the time
where the time goes in v5:
time: 75.8 us; the launch traced here: 74.7 us
  Pallas kernels  72.9 us (96%)
  local copies, waits for them, and re-layouts  1.82 us (2%)
    pallas_call x1, Pallas kernels, dense_plan(): pl.pallas_call(functools.partial(fused_kernel, nodes, locals_, capacity,...  72.9 us
    unnamed x1, local copies, waits for them, and re-layouts  1.82 us

profile of v5, /device:TPU:0, one launch (start us, length us, event | category | flops | bytes accessed | tf_op | source)
XLA Modules:
  0.0 74.7 jit_solution(4722373545588624462)
XLA Ops:
  0.0 72.9 %shard_map.55 = bf16[64,3584]{1,0:T(8,128)(2,1)} custom-call(f32[8,64]{1,0:T(8,128)} %bitcast.5, s32[4,64]{1,0:T(4,128)} %bitcast.7, s32[8,64]{1,0:T(8,128)} %bitcast.6, bf16[512,1024]{1,0:T(8,128)(2,1)} %bitcast.4, bf16[1,1024,3584]{2,1,0:T(8,128)(2,1)} %w_hbm.1), custom_call_target="tpu_custom_call" | custom-call | tf_op jit(solution)/shard_map/pallas_call | solution.py:343
  72.9 1.8 %copy.7 = bf16[64,3584]{1,0:T(8,128)(2,1)} copy(bf16[64,3584]{1,0:T(8,128)(2,1)} %shard_map.55) | data formatting | bytes 917504

commit v6 on v4

--- a/solution.py
+++ b/solution.py
@@ -178,10 +178,11 @@
             device_id={"node": me_n, "local": l_t}, device_id_type=MESH,
         )
 
-    for d in order:
-        for dl in range(locals_ - 1, -1, -1):
-            if d or dl:
-                hidden_copy(d, dl).start()
+    for k in range(0, nodes, 2):
+        for dl in (2, 1, 3, 0):
+            for d in order[k:k + 2]:
+                if d or dl:
+                    hidden_copy(d, dl).start()
     for dl in range(1, locals_):
         mix_copy(dl).start()
     xr[0, me_l] = xs[me_l * nodes + me_n]

time: 75.7 us -> 75.1 us (level); the launches traced: 74.7 us -> 74.9 us
  no operation moved by 1% of the time
where the time goes in v6:
time: 75.1 us; the launch traced here: 74.9 us
  Pallas kernels  73.1 us (97%)
  local copies, waits for them, and re-layouts  1.82 us (2%)
    pallas_call x1, Pallas kernels, dense_plan(): pl.pallas_call(functools.partial(fused_kernel, nodes, locals_, capacity,...  73.1 us
    unnamed x1, local copies, waits for them, and re-layouts  1.82 us

profile of v6, /device:TPU:0, one launch (start us, length us, event | category | flops | bytes accessed | tf_op | source)
XLA Modules:
  0.0 74.9 jit_solution(6662428145980763820)
XLA Ops:
  0.0 73.1 %shard_map.55 = bf16[64,3584]{1,0:T(8,128)(2,1)} custom-call(f32[8,64]{1,0:T(8,128)} %bitcast.5, s32[4,64]{1,0:T(4,128)} %bitcast.7, s32[8,64]{1,0:T(8,128)} %bitcast.6, bf16[512,1024]{1,0:T(8,128)(2,1)} %bitcast.4, bf16[1,1024,3584]{2,1,0:T(8,128)(2,1)} %w_hbm.1), custom_call_target="tpu_custom_call" | custom-call | tf_op jit(solution)/shard_map/pallas_call | solution.py:343
  73.1 1.8 %copy.7 = bf16[64,3584]{1,0:T(8,128)(2,1)} copy(bf16[64,3584]{1,0:T(8,128)(2,1)} %shard_map.55) | data formatting | bytes 917504

commit v7 on v6

--- a/solution.py
+++ b/solution.py
@@ -285,13 +285,14 @@
             for low in lows:
                 apply(c + ahead, low)
 
-        @pl.when(c > 0)
-        def _():
-            merge(c - 1)
+        @pl.when(c > 1)
+        def _():
+            merge(c - 2)
 
         return carry
 
     lax.fori_loop(0, chunks, combine_chunk, 0)
+    merge(chunks - 2)
     merge(chunks - 1)
 
     def final_chunk(c, carry):

time: 75.1 us -> 76.2 us (1.015)
  no operation moved by 1% of the time
where the time goes in v7:
time: 76.2 us; the launch traced here: 75.6 us
  Pallas kernels  73.8 us (97%)
  local copies, waits for them, and re-layouts  1.82 us (2%)
    pallas_call x1, Pallas kernels, dense_plan(): pl.pallas_call(functools.partial(fused_kernel, nodes, locals_, capacity,...  73.8 us
    unnamed x1, local copies, waits for them, and re-layouts  1.82 us

profile of v7, /device:TPU:0, one launch (start us, length us, event | category | flops | bytes accessed | tf_op | source)
XLA Modules:
  0.0 75.6 jit_solution(8121513478933999569)
XLA Ops:
  0.0 73.8 %shard_map.55 = bf16[64,3584]{1,0:T(8,128)(2,1)} custom-call(f32[8,64]{1,0:T(8,128)} %bitcast.5, s32[4,64]{1,0:T(4,128)} %bitcast.7, s32[8,64]{1,0:T(8,128)} %bitcast.6, bf16[512,1024]{1,0:T(8,128)(2,1)} %bitcast.4, bf16[1,1024,3584]{2,1,0:T(8,128)(2,1)} %w_hbm.1), custom_call_target="tpu_custom_call" | custom-call | tf_op jit(solution)/shard_map/pallas_call | solution.py:344
  73.8 1.8 %copy.7 = bf16[64,3584]{1,0:T(8,128)(2,1)} copy(bf16[64,3584]{1,0:T(8,128)(2,1)} %shard_map.55) | data formatting | bytes 917504
